TPU v7x, 512 devices: a whole 4x8x8 slice. The times are simulated.
512 devices in a mesh: rep: 4 (over x), ctx: 16 (over z, core), tp: 8 (over y).
Axes of the slice: x: 4, y: 8, z: 8, core: 2. Of those that a mesh axis runs over, the one named last changes fastest.
Arguments:
- q_arrived: bfloat16 [4, 6144, 4096], P('rep', 'ctx', 'tp'), may hold values from -6 to 6
- key_value_landed: bfloat16 [4, 6144, 2048], P('rep', 'ctx', 'tp'), may hold values from -6 to 6
- finish: int32 [48, 4], P('ctx'), may hold values from 0 to 3, as said below
- document_numbers: int32 [4, 6144], P('rep', 'ctx'), may hold values from 0 to 3, never falling along the last dimension, each value on 1 to 4608 neighbouring positions
Outputs:
- attended: bfloat16 [4, 6144, 4096], P('rep', 'ctx', 'tp')
Inputs may be any that keep to these rules, and one draw needn't show every extreme that they name: `finish`: each row is a permutation of the scoring groups. Within the blocks of one index of ctx, taken in aligned runs of 4 blocks, no arrival group sends two blocks of a run to the same scoring group, so one arrival group sends one scoring group at most 1 block of one index of ctx.
All inputs are finite; a program needn't handle non-finite values.
Results may differ from a plain program's by a relative error of at most 0.0038.
Values may be sent and summed in bfloat16 or wider, within the bound.
A program may use at most 64 MiB of HBM per device.

v0:
```python
import jax
import jax.numpy as jnp
from jax import lax
from jax.sharding import PartitionSpec as P

HEAD_SIZE = 128
ARRIVAL_TOKENS = 128


def score_tile(query_rows, key_tile):
    return jnp.einsum(
        "gqd,kd->gqk", query_rows, key_tile, preferred_element_type=jnp.float32
    ) * query_rows.shape[-1] ** (-0.5)


def visible_tile(query_pos, query_doc, key_pos, key_doc):
    return (
        (key_pos[None, :] >= 0)
        & (key_pos[None, :] <= query_pos[:, None])
        & (key_doc[None, :] == query_doc[:, None])
    )


def attend(query_rows, key_cols, value_cols, query_pos, query_doc, key_pos, key_doc, tile_len):
    tiles = key_cols.shape[0] // tile_len

    def pieces(tile_num):
        offset = tile_num * tile_len
        return (
            lax.dynamic_slice_in_dim(key_cols, offset, tile_len, 0),
            lax.dynamic_slice_in_dim(value_cols, offset, tile_len, 0),
            lax.dynamic_slice_in_dim(key_pos, offset, tile_len, 0),
            lax.dynamic_slice_in_dim(key_doc, offset, tile_len, 0),
        )

    def first_pass(tile_num, highest):
        key_tile, value_tile, pos_tile, doc_tile = pieces(tile_num)
        allowed = visible_tile(query_pos, query_doc, pos_tile, doc_tile)
        scores = jnp.where(allowed[None], score_tile(query_rows, key_tile), -1e30)
        return jnp.maximum(highest, jnp.max(scores, axis=-1))

    highest = lax.fori_loop(
        0, tiles, first_pass, jnp.full(query_rows.shape[:2], -1e30, jnp.float32)
    )

    def second_pass(tile_num, state_pair):
        denom_sum, summed = state_pair
        key_tile, value_tile, pos_tile, doc_tile = pieces(tile_num)
        allowed = visible_tile(query_pos, query_doc, pos_tile, doc_tile)
        scores = score_tile(query_rows, key_tile)
        weights = jnp.where(allowed[None], jnp.exp(scores - highest[..., None]), 0.0)
        denom_sum = denom_sum + jnp.sum(weights, axis=-1)
        summed = summed + jnp.einsum(
            "gqk,kd->gqd",
            weights.astype(jnp.bfloat16),
            value_tile,
            preferred_element_type=jnp.float32,
        )
        return (denom_sum, summed)

    start_pair = (
        jnp.zeros(query_rows.shape[:2], jnp.float32),
        jnp.zeros(query_rows.shape, jnp.float32),
    )
    denom_sum, summed = lax.fori_loop(0, tiles, second_pass, start_pair)
    return (summed / denom_sum[..., None]).astype(jnp.bfloat16)


def body(q_arrived, key_value_landed, finish, document_numbers):
    tok_rows = q_arrived.shape[1]
    q_width = q_arrived.shape[2]
    kv_width = key_value_landed.shape[2]
    block_list = tok_rows // ARRIVAL_TOKENS
    groups = lax.axis_size("rep")
    rep_place = lax.axis_index("rep")
    group_ids = jnp.arange(groups, dtype=jnp.int32)
    own_pick = group_ids[None, :] == rep_place
    own_col = jnp.sum(jnp.where(own_pick, finish, 0), axis=1)
    targets = (own_col[None, :] == group_ids[:, None])[:, :, None, None]

    def outgoing(row_data, col_count):
        shaped = row_data.reshape(block_list, ARRIVAL_TOKENS, col_count)
        return jnp.where(targets, shaped[None], jnp.zeros((), jnp.bfloat16))

    def arrived(received, col_count):
        return jnp.sum(received, axis=0).reshape(tok_rows, col_count)

    ctx_place = lax.axis_index("ctx")
    own_doc = document_numbers[0]
    query_pos = ctx_place * tok_rows + jnp.arange(tok_rows, dtype=jnp.int32)
    query_doc = own_doc.astype(jnp.float32)
    q_recv, kv_recv = (
        lax.all_to_all(
            outgoing(q_arrived, q_width), "rep", split_axis=0, concat_axis=0, tiled=True
        ),
        lax.all_to_all(
            outgoing(key_value_landed, kv_width), "rep", split_axis=0, concat_axis=0, tiled=True
        ),
    )
    doc_wire = own_doc.astype(jnp.bfloat16)
    keys_all = lax.all_gather(arrived(kv_recv, kv_width), "ctx", axis=0, tiled=True)
    docs_all = lax.all_gather(doc_wire, "ctx", axis=0, tiled=True)
    key_pos = jnp.arange(keys_all.shape[0], dtype=jnp.int32)
    keys_all, key_doc, key_pos = (keys_all, docs_all.astype(jnp.float32), key_pos)
    q_rows = arrived(q_recv, q_width)
    head_dim = HEAD_SIZE
    key_value_head_list = kv_width // (2 * head_dim)
    group_wise = q_width // (key_value_head_list * head_dim)
    query_rows = q_rows
    query_rows = query_rows.reshape(tok_rows, group_wise, head_dim).transpose(1, 0, 2)
    key_cols = keys_all[:, 0:head_dim]
    value_cols = keys_all[:, head_dim : 2 * head_dim]
    result = attend(
        query_rows, key_cols, value_cols, query_pos, query_doc, key_pos, key_doc, 2 * tok_rows
    )
    outputs = result.transpose(1, 0, 2).reshape(tok_rows, group_wise * head_dim)
    return outputs[None]


def solution(mesh):
    in_specs = (P("rep", "ctx", "tp"), P("rep", "ctx", "tp"), P("ctx", None), P("rep", "ctx"))
    out_specs = P("rep", "ctx", "tp")
    return jax.shard_map(body, mesh=mesh, in_specs=in_specs, out_specs=out_specs, check_vma=False)
```

profile of v0, /device:TPU:1, one launch (start us, length us, event | category | flops | bytes accessed | tf_op | source)
XLA Modules:
  0.0 167.5 jit_solution(9376043607335876298)
XLA Ops:
  8.5 13.0 %all_to_all.10 = bf16[4,3,128,256]{3,2,1,0:T(8,128)(2,1)S(1)} all-to-all(bf16[4,3,128,256]{3,2,1,0:T(8,128)(2,1)S(1)} %broadcast_select_fusion.1), channel_id=1, replica_groups=mesh['rep'=4,'ctx'=16,'tp'=8] {'rep'}, dimensions={0} | all-to-all | bytes 1572864 | tf_op jit(solution)/shard_map/all_to_all | solution.py:96
  23.7 3.6 %all-to-all-start.1 = ((bf16[4,3,128,512]{3,2,1,0:T(8,128)(2,1)}), bf16[4,3,128,512]{3,2,1,0:T(8,128)(2,1)S(1)}, u32[]{:S(2)}, u32[]{:S(2)}) async-start(bf16[4,3,128,512]{3,2,1,0:T(8,128)(2,1)} %broadcast_select_fusion), calls=%async_computation.1 | async-start | bytes 3145728 | tf_op jit(solution)/shard_map/all_to_all | solution.py:93
  27.3 27.9 %all-gather = bf16[1,6144]{1,0:T(2,128)(2,1)S(1)} all-gather(bf16[1,384]{1,0:T(2,128)(2,1)S(1)} %convert_element_type.29), channel_id=2, replica_groups=mesh['rep'=4,'ctx'=16,'tp'=8] {'ctx'}, dimensions={1}, use_global_device_ids=true | all-gather | bytes 13056 | tf_op jit(solution)/shard_map/all_gather | solution.py:102
  56.4 17.9 %all-gather.3.cloned.1.call-done = bf16[6144,256]{1,0:T(8,128)(2,1)} async-done(((bf16[384,256]{1,0:T(8,128)(2,1)}), bf16[6144,256]{1,0:T(8,128)(2,1)}) %all-gather.3.cloned.1.call-update) | async-done | bytes 3145744 | tf_op jit(solution)/shard_map/all_gather | solution.py:101
  74.4 2.1 %fusion.26 = (bf16[6144,128]{1,0:T(8,128)(2,1)S(1)}, bf16[6144,128]{1,0:T(8,128)(2,1)S(1)}) fusion(bf16[6144,256]{1,0:T(8,128)(2,1)} %all-gather.3.cloned.1.call-done), kind=kLoop, calls=%fused_computation.38 | loop fusion | bytes 6291456 | tf_op jit(solution)/shard_map/slice | solution.py:112
  77.1 27.7 %while.30 = (s32[]{:T(128)}, f32[4,384]{1,0:T(4,128)}, s32[6144]{0:T(1024)}, f32[6144]{0:T(1024)}, f32[384]{0:T(512)S(1)}, /*index=5*/bf16[6144,128]{1,0:T(8,128...) while((s32[]{:T(128)}, f32[4,384]{1,0:T(4,128)}, ...), condition=%wide.region_5.6_spmd.clone, body=%wide.region_3.5_spmd.clone.sunk | while | flops 306711168 | bytes 1278205 | solution.py:42
  105.4 52.7 %while.31 = (s32[]{:T(128)}, f32[4,384]{1,0:T(4,128)S(1)}, f32[4,384,128]{2,1,0:T(8,128)}, s32[6144]{0:T(1024)}, f32[6144]{0:T(1024)}, /*index=5*/f32[384]{0:T(5...) while((s32[]{:T(128)}, f32[4,384]{1,0:T(4,128)S(1)}, ...), condition=%wide.region_8.9_spmd.clone, body=%wide.region_6.8_spmd.clone.sunk | while | flops 614992512 | bytes 19058996 | solution.py:65
  107.3 2.2 %fusion.43 = (f32[4,384]{1,0:T(4,128)S(1)}, f32[768,4,384]{2,0,1:T(8,128)S(1)}) fusion(f32[4,384]{1,0:T(4,128)} %get-tuple-element.687, pred[384,768]{0,1:T(8,128)(4,1)S(1)} %compare_and_fusion.5, bf16[4,384,128]{2,1,0:T(8,128)(2,1)S(1)} %get-tuple-element.686, bf16[6144,128]{1,0:T(8,128)(2,1)S(1)} %get-tuple-element.685, s32[]{:T(128)S(6)} %select_n.76), kind=kOutput, calls=%fused_computation.13.clone.1 | convolution fusion | flops 306706944 | bytes 5615620 | tf_op jit(solution)/shard_map/while/body/eval_jaxpr/gqd,kd->gqk/dot_general | solution.py:11
  109.5 1.5 fusion.44
  113.9 2.2 %fusion.43 = (f32[4,384]{1,0:T(4,128)S(1)}, f32[768,4,384]{2,0,1:T(8,128)S(1)}) fusion(f32[4,384]{1,0:T(4,128)} %get-tuple-element.687, pred[384,768]{0,1:T(8,128)(4,1)S(1)} %compare_and_fusion.5, bf16[4,384,128]{2,1,0:T(8,128)(2,1)S(1)} %get-tuple-element.686, bf16[6144,128]{1,0:T(8,128)(2,1)S(1)} %get-tuple-element.685, s32[]{:T(128)S(6)} %select_n.76), kind=kOutput, calls=%fused_computation.13.clone.1 | convolution fusion | flops 306706944 | bytes 5615620 | tf_op jit(solution)/shard_map/while/body/eval_jaxpr/gqd,kd->gqk/dot_general | solution.py:11
  116.1 1.5 fusion.44
  120.5 2.2 %fusion.43 = (f32[4,384]{1,0:T(4,128)S(1)}, f32[768,4,384]{2,0,1:T(8,128)S(1)}) fusion(f32[4,384]{1,0:T(4,128)} %get-tuple-element.687, pred[384,768]{0,1:T(8,128)(4,1)S(1)} %compare_and_fusion.5, bf16[4,384,128]{2,1,0:T(8,128)(2,1)S(1)} %get-tuple-element.686, bf16[6144,128]{1,0:T(8,128)(2,1)S(1)} %get-tuple-element.685, s32[]{:T(128)S(6)} %select_n.76), kind=kOutput, calls=%fused_computation.13.clone.1 | convolution fusion | flops 306706944 | bytes 5615620 | tf_op jit(solution)/shard_map/while/body/eval_jaxpr/gqd,kd->gqk/dot_general | solution.py:11
  122.7 1.5 fusion.44
  127.1 2.2 %fusion.43 = (f32[4,384]{1,0:T(4,128)S(1)}, f32[768,4,384]{2,0,1:T(8,128)S(1)}) fusion(f32[4,384]{1,0:T(4,128)} %get-tuple-element.687, pred[384,768]{0,1:T(8,128)(4,1)S(1)} %compare_and_fusion.5, bf16[4,384,128]{2,1,0:T(8,128)(2,1)S(1)} %get-tuple-element.686, bf16[6144,128]{1,0:T(8,128)(2,1)S(1)} %get-tuple-element.685, s32[]{:T(128)S(6)} %select_n.76), kind=kOutput, calls=%fused_computation.13.clone.1 | convolution fusion | flops 306706944 | bytes 5615620 | tf_op jit(solution)/shard_map/while/body/eval_jaxpr/gqd,kd->gqk/dot_general | solution.py:11
  129.3 1.5 fusion.44
  133.7 2.2 %fusion.43 = (f32[4,384]{1,0:T(4,128)S(1)}, f32[768,4,384]{2,0,1:T(8,128)S(1)}) fusion(f32[4,384]{1,0:T(4,128)} %get-tuple-element.687, pred[384,768]{0,1:T(8,128)(4,1)S(1)} %compare_and_fusion.5, bf16[4,384,128]{2,1,0:T(8,128)(2,1)S(1)} %get-tuple-element.686, bf16[6144,128]{1,0:T(8,128)(2,1)S(1)} %get-tuple-element.685, s32[]{:T(128)S(6)} %select_n.76), kind=kOutput, calls=%fused_computation.13.clone.1 | convolution fusion | flops 306706944 | bytes 5615620 | tf_op jit(solution)/shard_map/while/body/eval_jaxpr/gqd,kd->gqk/dot_general | solution.py:11
  135.9 1.5 fusion.44
  140.3 2.2 %fusion.43 = (f32[4,384]{1,0:T(4,128)S(1)}, f32[768,4,384]{2,0,1:T(8,128)S(1)}) fusion(f32[4,384]{1,0:T(4,128)} %get-tuple-element.687, pred[384,768]{0,1:T(8,128)(4,1)S(1)} %compare_and_fusion.5, bf16[4,384,128]{2,1,0:T(8,128)(2,1)S(1)} %get-tuple-element.686, bf16[6144,128]{1,0:T(8,128)(2,1)S(1)} %get-tuple-element.685, s32[]{:T(128)S(6)} %select_n.76), kind=kOutput, calls=%fused_computation.13.clone.1 | convolution fusion | flops 306706944 | bytes 5615620 | tf_op jit(solution)/shard_map/while/body/eval_jaxpr/gqd,kd->gqk/dot_general | solution.py:11
  142.5 1.5 fusion.44
  146.9 2.2 %fusion.43 = (f32[4,384]{1,0:T(4,128)S(1)}, f32[768,4,384]{2,0,1:T(8,128)S(1)}) fusion(f32[4,384]{1,0:T(4,128)} %get-tuple-element.687, pred[384,768]{0,1:T(8,128)(4,1)S(1)} %compare_and_fusion.5, bf16[4,384,128]{2,1,0:T(8,128)(2,1)S(1)} %get-tuple-element.686, bf16[6144,128]{1,0:T(8,128)(2,1)S(1)} %get-tuple-element.685, s32[]{:T(128)S(6)} %select_n.76), kind=kOutput, calls=%fused_computation.13.clone.1 | convolution fusion | flops 306706944 | bytes 5615620 | tf_op jit(solution)/shard_map/while/body/eval_jaxpr/gqd,kd->gqk/dot_general | solution.py:11
  149.1 1.5 fusion.44
  153.4 2.2 %fusion.43 = (f32[4,384]{1,0:T(4,128)S(1)}, f32[768,4,384]{2,0,1:T(8,128)S(1)}) fusion(f32[4,384]{1,0:T(4,128)} %get-tuple-element.687, pred[384,768]{0,1:T(8,128)(4,1)S(1)} %compare_and_fusion.5, bf16[4,384,128]{2,1,0:T(8,128)(2,1)S(1)} %get-tuple-element.686, bf16[6144,128]{1,0:T(8,128)(2,1)S(1)} %get-tuple-element.685, s32[]{:T(128)S(6)} %select_n.76), kind=kOutput, calls=%fused_computation.13.clone.1 | convolution fusion | flops 306706944 | bytes 5615620 | tf_op jit(solution)/shard_map/while/body/eval_jaxpr/gqd,kd->gqk/dot_general | solution.py:11
  155.7 1.5 fusion.44
  158.1 1.4 fusion.25
  (194 shorter events, 57.9 us)
Async XLA Ops:
  6.5 15.8 %copy-start.2 = (bf16[1,384,512]{2,1,0:T(8,128)(2,1)S(1)}, bf16[1,384,512]{2,1,0:T(8,128)(2,1)}, u32[]{:S(2)}) copy-start(bf16[1,384,512]{2,1,0:T(8,128)(2,1)} %param.8) | copy-start | bytes 1179652
  6.5 67.8 %all-gather.3.cloned.1.call-start = ((), (), s32[]{:S(2)}) async-start(), calls=%async_computation.2 | async-start | bytes 3342336 | tf_op jit(solution)/shard_map/all_gather | solution.py:101
  22.3 5.0 %copy-start.6 = (s32[1,384]{1,0:T(1,128)S(1)}, s32[1,384]{1,0:T(1,128)}, u32[]{:S(2)}) copy-start(s32[1,384]{1,0:T(1,128)} %param.11) | copy-start | bytes 4612
  23.7 32.2 %all-to-all-start.1 = ((bf16[4,3,128,512]{3,2,1,0:T(8,128)(2,1)}), bf16[4,3,128,512]{3,2,1,0:T(8,128)(2,1)S(1)}, u32[]{:S(2)}, u32[]{:S(2)}) async-start(bf16[4,3,128,512]{3,2,1,0:T(8,128)(2,1)} %broadcast_select_fusion), calls=%async_computation.1 | async-start | bytes 3145728 | tf_op jit(solution)/shard_map/all_to_all | solution.py:93
  103.2 0.9 copy-start.3
  107.3 2.2 %copy-start = (f32[4,384,128]{2,1,0:T(8,128)S(1)}, f32[4,384,128]{2,1,0:T(8,128)}, u32[]{:S(2)}) copy-start(f32[4,384,128]{2,1,0:T(8,128)} %get-tuple-element.666) | copy-start | bytes 2359300 | tf_op jit(solution)/shard_map/while
  107.3 2.2 %copy-start.5 = (f32[4,384]{1,0:T(4,128)S(1)}, f32[4,384]{1,0:T(4,128)}, u32[]{:S(2)}) copy-start(f32[4,384]{1,0:T(4,128)} %get-tuple-element.687) | copy-start | bytes 18436 | tf_op jit(solution)/shard_map/while
  113.9 2.2 %copy-start = (f32[4,384,128]{2,1,0:T(8,128)S(1)}, f32[4,384,128]{2,1,0:T(8,128)}, u32[]{:S(2)}) copy-start(f32[4,384,128]{2,1,0:T(8,128)} %get-tuple-element.666) | copy-start | bytes 2359300 | tf_op jit(solution)/shard_map/while
  113.9 2.2 %copy-start.5 = (f32[4,384]{1,0:T(4,128)S(1)}, f32[4,384]{1,0:T(4,128)}, u32[]{:S(2)}) copy-start(f32[4,384]{1,0:T(4,128)} %get-tuple-element.687) | copy-start | bytes 18436 | tf_op jit(solution)/shard_map/while
  120.5 2.2 %copy-start = (f32[4,384,128]{2,1,0:T(8,128)S(1)}, f32[4,384,128]{2,1,0:T(8,128)}, u32[]{:S(2)}) copy-start(f32[4,384,128]{2,1,0:T(8,128)} %get-tuple-element.666) | copy-start | bytes 2359300 | tf_op jit(solution)/shard_map/while
  120.5 2.2 %copy-start.5 = (f32[4,384]{1,0:T(4,128)S(1)}, f32[4,384]{1,0:T(4,128)}, u32[]{:S(2)}) copy-start(f32[4,384]{1,0:T(4,128)} %get-tuple-element.687) | copy-start | bytes 18436 | tf_op jit(solution)/shard_map/while
  124.2 0.9 copy-start.1
  127.1 2.2 %copy-start = (f32[4,384,128]{2,1,0:T(8,128)S(1)}, f32[4,384,128]{2,1,0:T(8,128)}, u32[]{:S(2)}) copy-start(f32[4,384,128]{2,1,0:T(8,128)} %get-tuple-element.666) | copy-start | bytes 2359300 | tf_op jit(solution)/shard_map/while
  127.1 2.2 %copy-start.5 = (f32[4,384]{1,0:T(4,128)S(1)}, f32[4,384]{1,0:T(4,128)}, u32[]{:S(2)}) copy-start(f32[4,384]{1,0:T(4,128)} %get-tuple-element.687) | copy-start | bytes 18436 | tf_op jit(solution)/shard_map/while
  133.7 2.2 %copy-start = (f32[4,384,128]{2,1,0:T(8,128)S(1)}, f32[4,384,128]{2,1,0:T(8,128)}, u32[]{:S(2)}) copy-start(f32[4,384,128]{2,1,0:T(8,128)} %get-tuple-element.666) | copy-start | bytes 2359300 | tf_op jit(solution)/shard_map/while
  133.7 2.2 %copy-start.5 = (f32[4,384]{1,0:T(4,128)S(1)}, f32[4,384]{1,0:T(4,128)}, u32[]{:S(2)}) copy-start(f32[4,384]{1,0:T(4,128)} %get-tuple-element.687) | copy-start | bytes 18436 | tf_op jit(solution)/shard_map/while
  140.3 2.2 %copy-start = (f32[4,384,128]{2,1,0:T(8,128)S(1)}, f32[4,384,128]{2,1,0:T(8,128)}, u32[]{:S(2)}) copy-start(f32[4,384,128]{2,1,0:T(8,128)} %get-tuple-element.666) | copy-start | bytes 2359300 | tf_op jit(solution)/shard_map/while
  140.3 2.2 %copy-start.5 = (f32[4,384]{1,0:T(4,128)S(1)}, f32[4,384]{1,0:T(4,128)}, u32[]{:S(2)}) copy-start(f32[4,384]{1,0:T(4,128)} %get-tuple-element.687) | copy-start | bytes 18436 | tf_op jit(solution)/shard_map/while
  146.9 2.2 %copy-start = (f32[4,384,128]{2,1,0:T(8,128)S(1)}, f32[4,384,128]{2,1,0:T(8,128)}, u32[]{:S(2)}) copy-start(f32[4,384,128]{2,1,0:T(8,128)} %get-tuple-element.666) | copy-start | bytes 2359300 | tf_op jit(solution)/shard_map/while
  146.9 2.2 %copy-start.5 = (f32[4,384]{1,0:T(4,128)S(1)}, f32[4,384]{1,0:T(4,128)}, u32[]{:S(2)}) copy-start(f32[4,384]{1,0:T(4,128)} %get-tuple-element.687) | copy-start | bytes 18436 | tf_op jit(solution)/shard_map/while
  150.6 0.9 copy-start.1
  153.4 2.2 %copy-start = (f32[4,384,128]{2,1,0:T(8,128)S(1)}, f32[4,384,128]{2,1,0:T(8,128)}, u32[]{:S(2)}) copy-start(f32[4,384,128]{2,1,0:T(8,128)} %get-tuple-element.666) | copy-start | bytes 2359300 | tf_op jit(solution)/shard_map/while
  153.4 2.2 %copy-start.5 = (f32[4,384]{1,0:T(4,128)S(1)}, f32[4,384]{1,0:T(4,128)}, u32[]{:S(2)}) copy-start(f32[4,384]{1,0:T(4,128)} %get-tuple-element.687) | copy-start | bytes 18436 | tf_op jit(solution)/shard_map/while
  157.2 0.9 copy-start.1
  (20 other events, 15.7 us)
Sparse Core Ops, SparseCore 0:
  22.4 51.9 all-gather.2
where the time goes:
time: 170 us; the launch traced here: 168 us
  blocking collectives  40.9 us (24%)
  matrix products  36.6 us (22%)
  local copies, waits for them, and re-layouts  28.9 us (17%)
  other arithmetic  25.3 us (15%)
  waiting for transfers between devices  17.9 us (11%)
  between operations  13.5 us (8%)
  starting transfers between devices  3.56 us (2%)
    all_gather x1, blocking collectives, body(): docs_all = lax.all_gather(doc_wire, 'ctx', axis=0, tiled=True)  27.9 us
    dot_general x16, matrix products, score_tile(): jnp.einsum('gqd,kd->gqk', query_rows, key_tile, preferred_element_type=jn...  24.6 us
    all_gather x1, waiting for transfers between devices, body(): lax.all_gather(arrived(kv_recv, kv_width), 'ctx', axis=0, tiled=True)  17.9 us
    all_to_all x1, blocking collectives, body(): lax.all_to_all(outgoing(key_value_landed, kv_width), 'rep', split_axis=0,...  13 us
    ge x16, other arithmetic, visible_tile(): key_pos[None, :] >= 0  12.3 us
    dynamic_slice x16, local copies, waits for them, and re-layouts, pieces(): lax.dynamic_slice_in_dim(key_doc, offset, tile_len, 0)  12.3 us
    while x80, local copies, waits for them, and re-layouts  12 us
    dot_general x8, matrix products, second_pass(): jnp.einsum('gqk,kd->gqd', weights.astype(jnp.bfloat16), value_tile, prefe...  12 us
  transfers between devices with their start and end apart: 2, of which 1 were waited for; matrix products, arithmetic and copies ran while one was open for 2% of the time, Pallas kernels for 0%

commit v1 on v0

v1 whole, which is shorter than its diff:
```python
import functools

import jax
import jax.numpy as jnp
from jax import lax
from jax.experimental import pallas as pl
from jax.experimental.pallas import tpu as pltpu
from jax.sharding import PartitionSpec as P

HEAD = 128
BLOCK = 128
UP = 4
DOWN = 3
PIECES = 2
SCALE = HEAD**-0.5 * 1.4426950408889634
HIDE = -float(2**20)
MESH = pl.DeviceIdType.MESH


def kernel(
    reps, ctxs, q_hbm, kv_hbm, fin_hbm, doc_hbm, out_hbm,
    q_in, kv_in, fin, doc, send_kv, send_q, recv_kv, recv_q, kvs, counts, hide, qa, top, acc, out,
    in_sem, x_send, x_recv, cnt_send, cnt_recv, up_send, up_recv, dn_send, dn_recv,
    sib_send, sib_recv, out_sem,
):
    blocks = q_in.shape[0]
    rows = blocks * BLOCK
    heads = q_in.shape[2] // HEAD
    chips = ctxs // 2
    piece = rows // PIECES
    r = lax.axis_index("rep")
    c = lax.axis_index("ctx")
    z = c // 2
    core = c % 2
    above = {"ctx": (c + 2) % ctxs}
    below = {"ctx": (c + ctxs - 2) % ctxs}
    sibling = {"ctx": c + 1 - 2 * core}

    loads = [
        pltpu.make_async_copy(src, dst, in_sem.at[i])
        for i, (src, dst) in enumerate(
            [(fin_hbm, fin), (kv_hbm, kv_in), (q_hbm, q_in), (doc_hbm, doc)]
        )
    ]
    for load in loads:
        load.start()
    barrier = pltpu.get_barrier_semaphore()
    for step in range(1, reps):
        pl.semaphore_signal(barrier, inc=1, device_id={"rep": (r + step) % reps}, device_id_type=MESH)

    def greet(step, _):
        pl.semaphore_signal(barrier, inc=1, device_id={"ctx": (c + step) % ctxs}, device_id_type=MESH)
        return 0

    lax.fori_loop(1, ctxs, greet, 0)

    def block_for(group):
        found = jnp.int32(0)
        for b in range(1, blocks):
            found = jnp.where(fin[b, r] == group, b, found)
        return found

    def source_slot(b):
        source = jnp.int32(0)
        for s in range(1, reps):
            source = jnp.where(fin[b, s] == r, s, source)
        return (r + reps - source) % reps

    def exchange(step, which, src, dst):
        return pltpu.make_async_remote_copy(
            src_ref=src.at[step], dst_ref=dst.at[step],
            send_sem=x_send.at[which, step], recv_sem=x_recv.at[which, step],
            device_id={"rep": (r + step) % reps}, device_id_type=MESH,
        )

    loads[0].wait()
    loads[1].wait()
    targets = [block_for((r + step) % reps) for step in range(reps)]
    for step in range(1, reps):
        send_kv[step] = kv_in[targets[step]]
    pl.semaphore_wait(barrier, reps - 1 + ctxs - 1)
    for step in range(1, reps):
        exchange(step, 0, send_kv, recv_kv).start()
    loads[2].wait()
    for step in range(1, reps):
        send_q[step] = q_in[targets[step]]
        exchange(step, 1, send_q, recv_q).start()
    loads[3].wait()
    doc_row = doc[...]
    lane = lax.broadcasted_iota(jnp.int32, (8, HEAD), 1)
    before = jnp.zeros((8, HEAD), jnp.float32)
    numbers = 4
    for j in range(1, numbers):
        count = jnp.sum((doc_row < j).astype(jnp.float32), axis=1, keepdims=True)
        before = before + jnp.where(lane == j, count, 0.0)
    before = before + jnp.where(lane >= numbers, float(rows), 0.0)
    counts[c] = before

    def count_copy(step):
        return pltpu.make_async_remote_copy(
            src_ref=counts.at[c], dst_ref=counts.at[c],
            send_sem=cnt_send.at[step], recv_sem=cnt_recv.at[step],
            device_id={"ctx": (c + step) % ctxs}, device_id_type=MESH,
        )

    def send_counts(step, _):
        count_copy(step).start()
        return 0

    lax.fori_loop(1, ctxs, send_counts, 0)
    recv_kv[0] = kv_in[targets[0]]
    recv_q[0] = q_in[targets[0]]

    for step in range(1, reps):
        exchange(step, 0, send_kv, recv_kv).wait_recv()
    slots = [source_slot(b) for b in range(blocks)]
    for b in range(blocks):
        kvs[z, pl.ds(pl.multiple_of(core * rows + b * BLOCK, BLOCK), BLOCK), :] = recv_kv[slots[b]]

    def hop(slot, part, k, device, send, recv):
        where = kvs.at[slot, pl.ds(pl.multiple_of(core * rows + part * piece, piece), piece), :]
        return pltpu.make_async_remote_copy(
            src_ref=where, dst_ref=where, send_sem=send.at[k, part], recv_sem=recv.at[k, part],
            device_id=device, device_id_type=MESH,
        )

    def up(slot, part, k):
        return hop(slot, part, k, above, up_send, up_recv)

    def dn(slot, part, k):
        return hop(slot, part, k, below, dn_send, dn_recv)

    def sib(slot, part, k):
        return hop(slot, part, k, sibling, sib_send, sib_recv)

    for part in range(PIECES):
        @pl.when(z < chips - 1)
        def _():
            up(z, part, 1).start()

        @pl.when(z < chips - UP - 1)
        def _():
            dn(z, part, 1).start()

        @pl.when(core == 0)
        def _():
            sib(z, part, 0).start()

    def wait_counts(step, _):
        count_copy(step).wait()
        return 0

    lax.fori_loop(1, ctxs, wait_counts, 0)
    starts = counts[0]
    for i in range(1, ctxs):
        starts = starts + counts[i]
    starts = starts[0:1, :]
    ends = jnp.concatenate([starts[:, 1:], starts[:, HEAD - 1 :]], axis=1)

    def within(first, length):
        at = (lax.broadcasted_iota(jnp.int32, (length, HEAD), 0) + first).astype(jnp.float32)
        return (at >= starts) & (at < ends)

    def fill(slot, _):
        hide[slot] = jnp.where(within(slot * 2 * rows, 2 * rows), 0.0, HIDE).astype(jnp.bfloat16)
        return 0

    lax.fori_loop(0, z + 1, fill, 0)
    own_doc = jnp.where(within(c * rows, rows), 1.0, 0.0).astype(jnp.bfloat16)
    for h in range(heads):
        qa[h * rows : (h + 1) * rows, HEAD:] = own_doc
    for step in range(1, reps):
        exchange(step, 1, send_q, recv_q).wait_recv()
    for b in range(blocks):
        q_block = recv_q[slots[b]]
        for h in range(heads):
            qa[h * rows + b * BLOCK : h * rows + (b + 1) * BLOCK, 0:HEAD] = q_block[:, h * HEAD : (h + 1) * HEAD]

    def unit(slot, first, keys, diagonal):
        span = pl.ds(pl.multiple_of(first, BLOCK), keys)
        key_rows = jnp.concatenate([kvs[slot, span, 0:HEAD], hide[slot, span, :]], axis=1)
        value = kvs[slot, span, HEAD:]
        value_rows = jnp.concatenate([value, jnp.ones_like(value)], axis=1)

        def score(h):
            s = lax.dot_general(
                qa[h * rows : (h + 1) * rows, :], key_rows, (((1,), (1,)), ((), ())),
                preferred_element_type=jnp.float32,
            )
            if diagonal:
                ahead = lax.broadcasted_iota(jnp.int32, s.shape, 1) > lax.broadcasted_iota(jnp.int32, s.shape, 0)
                s = jnp.where(ahead, HIDE, s)
            return s

        def soften(h, s):
            part = slice(h * rows, (h + 1) * rows)
            high = jnp.max(s, axis=1, keepdims=True)
            if diagonal:
                now = jnp.broadcast_to(high, (rows, HEAD))
                decay = None
            else:
                now = jnp.maximum(top[part, :], high)
                decay = jnp.exp2((top[part, :] - now) * SCALE)
            top[part, :] = now
            p = jnp.exp2((s - jnp.concatenate([now] * (keys // HEAD), axis=1)) * SCALE)
            return p.astype(jnp.bfloat16), decay

        def mix(h, p, decay):
            part = slice(h * rows, (h + 1) * rows)
            o = jnp.dot(p, value_rows, preferred_element_type=jnp.float32)
            if diagonal:
                acc[part, :] = o
            else:
                acc[part, :] = acc[part, :] * jnp.concatenate([decay] * 2, axis=1) + o

        scores = {0: score(0)}
        soft = {}
        for h in range(heads + 1):
            if h + 1 < heads:
                scores[h + 1] = score(h + 1)
            if h < heads:
                soft[h] = soften(h, scores.pop(h))
            if h >= 1:
                mix(h - 1, *soft.pop(h - 1))

    unit(z, core * rows, rows, True)

    @pl.when(core == 1)
    def _():
        for part in range(PIECES):
            hop_in(kvs, sib_recv, z, 1 - core, part, 0, rows, piece, sib_send, sibling).wait_recv()
        unit(z, 0, rows, False)

    def receive(k, _):
        slot = (z + chips - k) % chips
        far = (z + k) % chips
        has_up = z >= k
        has_dn = (far < chips - UP - 1) & (k <= DOWN)
        use_dn = has_dn & (z > UP) & (z - far <= chips - 2)
        for part in range(PIECES):
            @pl.when(has_up)
            def _():
                up(slot, part, k).wait_recv()

                @pl.when((k < UP) & (z < chips - 1))
                def _():
                    up(slot, part, k + 1).start()

                sib(slot, part, k).start()

            @pl.when(has_dn)
            def _():
                dn(far, part, k).wait_recv()

                @pl.when(k < DOWN)
                def _():
                    dn(far, part, k + 1).start()

            @pl.when(use_dn)
            def _():
                sib(far, part, UP + k).start()

        @pl.when(has_up)
        def _():
            for part in range(PIECES):
                hop_in(kvs, sib_recv, slot, 1 - core, part, k, rows, piece, sib_send, sibling).wait_recv()
            unit(slot, 0, 2 * rows, False)

        @pl.when(use_dn)
        def _():
            for part in range(PIECES):
                hop_in(kvs, sib_recv, far, 1 - core, part, UP + k, rows, piece, sib_send, sibling).wait_recv()
            unit(far, 0, 2 * rows, False)

        return 0

    lax.fori_loop(1, UP + 1, receive, 0)

    for h in range(heads):
        part = slice(h * rows, (h + 1) * rows)
        out[:, h * HEAD : (h + 1) * HEAD] = (acc[part, 0:HEAD] / acc[part, HEAD:]).astype(jnp.bfloat16)
    result = pltpu.make_async_copy(out, out_hbm.at[0], out_sem)
    result.start()

    for step in range(1, reps):
        exchange(step, 0, send_kv, recv_kv).wait_send()
        exchange(step, 1, send_q, recv_q).wait_send()

    def drain(k, _):
        slot = (z + chips - k) % chips
        far = (z + k) % chips
        has_up = z >= k
        has_dn = (far < chips - UP - 1) & (k <= DOWN)
        use_dn = has_dn & (z > UP) & (z - far <= chips - 2)
        for part in range(PIECES):
            @pl.when(has_up)
            def _():
                @pl.when((k < UP) & (z < chips - 1))
                def _():
                    up(slot, part, k + 1).wait_send()

                sib(slot, part, k).wait_send()

            @pl.when(has_dn & (k < DOWN))
            def _():
                dn(far, part, k + 1).wait_send()

            @pl.when(use_dn)
            def _():
                sib(far, part, UP + k).wait_send()

        return 0

    lax.fori_loop(1, UP + 1, drain, 0)
    for part in range(PIECES):
        @pl.when(z < chips - 1)
        def _():
            up(z, part, 1).wait_send()

        @pl.when(z < chips - UP - 1)
        def _():
            dn(z, part, 1).wait_send()

        @pl.when(core == 0)
        def _():
            sib(z, part, 0).wait_send()

    result.wait()


def hop_in(kvs, recv, slot, core, part, k, rows, piece, send, device):
    where = kvs.at[slot, pl.ds(pl.multiple_of(core * rows + part * piece, piece), piece), :]
    return pltpu.make_async_remote_copy(
        src_ref=where, dst_ref=where, send_sem=send.at[k, part], recv_sem=recv.at[k, part],
        device_id=device, device_id_type=MESH,
    )


def body(q_arrived, key_value_landed, finish, document_numbers):
    rows, q_width = q_arrived.shape[1:]
    kv_width = key_value_landed.shape[2]
    reps = lax.axis_size("rep")
    ctxs = lax.axis_size("ctx")
    chips = ctxs // 2
    heads = q_width // HEAD
    blocks = rows // BLOCK
    bf16, f32 = jnp.bfloat16, jnp.float32
    dma = pltpu.SemaphoreType.DMA
    return pl.pallas_call(
        functools.partial(kernel, reps, ctxs),
        out_shape=jax.ShapeDtypeStruct(q_arrived.shape, bf16),
        in_specs=[pl.BlockSpec(memory_space=pl.ANY)] * 4,
        out_specs=pl.BlockSpec(memory_space=pl.ANY),
        scratch_shapes=[
            pltpu.VMEM((blocks, BLOCK, q_width), bf16),
            pltpu.VMEM((blocks, BLOCK, kv_width), bf16),
            pltpu.SMEM(finish.shape, jnp.int32),
            pltpu.VMEM(document_numbers.shape, jnp.int32),
            pltpu.VMEM((reps, BLOCK, kv_width), bf16),
            pltpu.VMEM((reps, BLOCK, q_width), bf16),
            pltpu.VMEM((reps, BLOCK, kv_width), bf16),
            pltpu.VMEM((reps, BLOCK, q_width), bf16),
            pltpu.VMEM((chips, 2 * rows, kv_width), bf16),
            pltpu.VMEM((ctxs, 8, HEAD), f32),
            pltpu.VMEM((chips, 2 * rows, HEAD), bf16),
            pltpu.VMEM((heads * rows, 2 * HEAD), bf16),
            pltpu.VMEM((heads * rows, HEAD), f32),
            pltpu.VMEM((heads * rows, 2 * HEAD), f32),
            pltpu.VMEM((rows, q_width), bf16),
            dma((4,)),
            dma((2, reps)),
            dma((2, reps)),
            dma((ctxs,)),
            dma((ctxs,)),
            dma((UP + 1, PIECES)),
            dma((UP + 1, PIECES)),
            dma((DOWN + 1, PIECES)),
            dma((DOWN + 1, PIECES)),
            dma((UP + DOWN + 1, PIECES)),
            dma((UP + DOWN + 1, PIECES)),
            dma,
        ],
        compiler_params=pltpu.CompilerParams(
            collective_id=0, has_side_effects=True, vmem_limit_bytes=48 * 2**20
        ),
    )(
        q_arrived.reshape(blocks, BLOCK, q_width),
        key_value_landed.reshape(blocks, BLOCK, kv_width),
        finish,
        document_numbers,
    )


def solution(mesh):
    in_specs = (P("rep", "ctx", "tp"), P("rep", "ctx", "tp"), P("ctx", None), P("rep", "ctx"))
    out_specs = P("rep", "ctx", "tp")
    return jax.shard_map(body, mesh=mesh, in_specs=in_specs, out_specs=out_specs, check_vma=False)
```

time: 170 us -> 43.5 us (0.26)
  the two profiles are of different devices: /device:TPU:1 before, /device:TPU:337 now
where the time goes in v1:
time: 43.5 us; the launch traced here: 43.3 us
  Pallas kernels  39.9 us (92%)
  local copies, waits for them, and re-layouts  3.37 us (8%)
    pallas_call x1, Pallas kernels, body(): pl.pallas_call(functools.partial(kernel, reps, ctxs), out_shape=jax.Shape...  39.9 us
    unnamed x9, local copies, waits for them, and re-layouts  3.37 us

profile of v1, /device:TPU:337, one launch (start us, length us, event | category | flops | bytes accessed | tf_op | source)
XLA Modules:
  0.0 43.3 jit_solution(8858950030038521266)
XLA Ops:
  0.0 0.0 copy-start.3
  0.0 0.0 copy-start.2
  0.0 0.7 %copy-done.3 = s32[1,384]{1,0:T(1,128)S(1)} copy-done((s32[1,384]{1,0:T(1,128)S(1)}, s32[1,384]{1,0:T(1,128)}, u32[]{:S(2)}) %copy-start.3) | copy-done | bytes 1560
  0.7 0.0 copy-done.2
  0.7 0.0 copy-start
  0.7 1.0 %copy-done = bf16[1,384,512]{2,1,0:T(8,128)(2,1)S(1)} copy-done((bf16[1,384,512]{2,1,0:T(8,128)(2,1)S(1)}, bf16[1,384,512]{2,1,0:T(8,128)(2,1)}, u32[]{:S(2)}) %copy-start) | copy-done | bytes 393240
  1.7 0.0 copy-start.1
  1.7 0.9 %copy-done.1 = bf16[1,384,256]{2,1,0:T(8,128)(2,1)S(1)} copy-done((bf16[1,384,256]{2,1,0:T(8,128)(2,1)S(1)}, bf16[1,384,256]{2,1,0:T(8,128)(2,1)}, u32[]{:S(2)}) %copy-start.1) | copy-done | bytes 196632
  2.6 39.9 %shard_map.46 = bf16[1,384,512]{2,1,0:T(8,128)(2,1)S(1)} custom-call(bf16[3,128,512]{2,1,0:T(8,128)(2,1)S(1)} %bitcast.2, bf16[3,128,256]{2,1,0:T(8,128)(2,1)S(1)} %bitcast.3, s32[3,4]{1,0:T(4,128)S(1)} %copy-done.2, s32[1,384]{1,0:T(1,128)S(1)} %copy-done.3), custom_call_target="tpu_custom_call" | custom-call | tf_op jit(solution)/shard_map/pallas_call | solution.py:349
  42.6 0.7 %copy.6 = bf16[1,384,512]{2,1,0:T(8,128)(2,1)} copy(bf16[1,384,512]{2,1,0:T(8,128)(2,1)S(1)} %shard_map.46) | data formatting | bytes 786432
Async XLA Ops:
  0.0 0.7 %copy-start.3 = (s32[1,384]{1,0:T(1,128)S(1)}, s32[1,384]{1,0:T(1,128)}, u32[]{:S(2)}) copy-start(s32[1,384]{1,0:T(1,128)} %doc_hbm.1) | copy-start | bytes 4612
  0.0 0.7 %copy-start.2 = (s32[3,4]{1,0:T(4,128)S(1)}, s32[3,4]{1,0:T(4,128)}, u32[]{:S(2)}) copy-start(s32[3,4]{1,0:T(4,128)} %fin_hbm.1) | copy-start | bytes 148
  0.7 1.0 %copy-start = (bf16[1,384,512]{2,1,0:T(8,128)(2,1)S(1)}, bf16[1,384,512]{2,1,0:T(8,128)(2,1)}, u32[]{:S(2)}) copy-start(bf16[1,384,512]{2,1,0:T(8,128)(2,1)} %param.4) | copy-start | bytes 1179652
  1.7 0.9 %copy-start.1 = (bf16[1,384,256]{2,1,0:T(8,128)(2,1)S(1)}, bf16[1,384,256]{2,1,0:T(8,128)(2,1)}, u32[]{:S(2)}) copy-start(bf16[1,384,256]{2,1,0:T(8,128)(2,1)} %param.5) | copy-start | bytes 589828

commit v2 on v1

v2 whole, which is shorter than its diff:
```python
import functools

import jax
import jax.numpy as jnp
from jax import lax
from jax.experimental import pallas as pl
from jax.experimental.pallas import tpu as pltpu
from jax.sharding import PartitionSpec as P

HEAD = 128
BLOCK = 128
NOTE = 16
NUMBERS = 4
UP = 4
PARTS = 2
SCALE = HEAD**-0.5 * 1.4426950408889634
HIDE = -float(2**20)
MESH = pl.DeviceIdType.MESH


def kernel(
    reps, ctxs, q_hbm, kv_hbm, fin_hbm, doc_hbm, out_hbm,
    q_in, kv_in, fin, doc, send_kv, send_q, recv_kv, recv_q, kvs, qa, top, acc, out,
    in_sem, x_send, x_recv, ready, up_send, up_recv, far_send, far_recv, sib_send, sib_recv, out_sem,
):
    blocks = q_in.shape[0]
    rows = blocks * BLOCK
    span = rows + NOTE
    heads = q_in.shape[2] // HEAD
    chips = ctxs // 2
    last = chips - 1
    half_rows = rows // PARTS
    pieces = [(p * half_rows, half_rows + (NOTE if p == PARTS - 1 else 0)) for p in range(PARTS)]
    r = lax.axis_index("rep")
    c = lax.axis_index("ctx")
    z = c // 2
    core = c % 2

    def on_chip(chip):
        return {"ctx": chip * 2 + core}

    above = on_chip((z + 1) % chips)
    below = on_chip((z + last) % chips)
    sibling = {"ctx": c + 1 - 2 * core}

    def signal(sem, device):
        pl.semaphore_signal(sem, inc=1, device_id=device, device_id_type=MESH)

    loads = [
        pltpu.make_async_copy(src, dst, in_sem.at[i])
        for i, (src, dst) in enumerate([(fin_hbm, fin), (kv_hbm, kv_in), (q_hbm, q_in), (doc_hbm, doc)])
    ]
    for load in loads:
        load.start()
    barrier = pltpu.get_barrier_semaphore()
    for step in range(1, reps):
        signal(barrier, {"rep": (r + step) % reps})
    signal(barrier, sibling)

    @pl.when(z < last)
    def _():
        signal(barrier, above)

    @pl.when(z == 0)
    def _():
        for chip in (2, last - 1, last):
            signal(barrier, on_chip(chip))

    def block_for(group):
        found = jnp.int32(0)
        for b in range(1, blocks):
            found = jnp.where(fin[b, r] == group, b, found)
        return found

    def source_slot(b):
        source = jnp.int32(0)
        for s in range(1, reps):
            source = jnp.where(fin[b, s] == r, s, source)
        return (r + reps - source) % reps

    def exchange(step, which, src, dst):
        return pltpu.make_async_remote_copy(
            src_ref=src.at[step], dst_ref=dst.at[step],
            send_sem=x_send.at[which, step], recv_sem=x_recv.at[which, step],
            device_id={"rep": (r + step) % reps}, device_id_type=MESH,
        )

    loads[0].wait()
    loads[1].wait()
    targets = [block_for((r + step) % reps) for step in range(reps)]
    for step in range(1, reps):
        send_kv[step] = kv_in[targets[step]]
    pl.semaphore_wait(
        barrier,
        reps + jnp.where(z > 0, 1, 0) + jnp.where((z == 2) | (z >= last - 1), 1, 0),
    )
    @pl.when(z > 0)
    def _():
        signal(ready.at[0], below)

    @pl.when(z == last - 1)
    def _():
        signal(ready.at[1], on_chip(0))

    @pl.when(z == last)
    def _():
        signal(ready.at[2], on_chip(0))

    for step in range(1, reps):
        exchange(step, 0, send_kv, recv_kv).start()
    loads[2].wait()
    for step in range(1, reps):
        send_q[step] = q_in[targets[step]]
        exchange(step, 1, send_q, recv_q).start()
    loads[3].wait()
    doc_row = doc[...]
    lane = lax.broadcasted_iota(jnp.int32, (NOTE, HEAD), 1)
    starts = jnp.where(lane >= NUMBERS, float(rows), 0.0)
    ends = jnp.where(lane >= NUMBERS - 1, float(rows), 0.0)
    for j in range(1, NUMBERS):
        count = jnp.sum((doc_row < j).astype(jnp.float32), axis=1, keepdims=True)
        starts = starts + jnp.where(lane == j, count, 0.0)
        ends = ends + jnp.where(lane == j - 1, count, 0.0)

    def in_two(count):
        most = float(rows // 2)
        line = lax.broadcasted_iota(jnp.int32, (NOTE, HEAD), 0)
        low = jnp.minimum(count, most)
        return jnp.where(line == 0, low, jnp.where(line == 1, count - low, 0.0)).astype(jnp.bfloat16)

    def place(half, first, length):
        return pl.ds(pl.multiple_of(half * span + first, 16), length)

    kvs[z, place(core, rows, NOTE), 0:HEAD] = in_two(starts)
    kvs[z, place(core, rows, NOTE), HEAD:] = in_two(ends)

    def within(starts, ends):
        at = lax.broadcasted_iota(jnp.int32, (rows, HEAD), 0).astype(jnp.float32)
        return (at >= starts) & (at < ends)

    own_doc = jnp.where(within(starts[0:1, :], ends[0:1, :]), 1.0, 0.0).astype(jnp.bfloat16)
    for h in range(heads):
        qa[h * rows : (h + 1) * rows, HEAD:] = own_doc
    recv_kv[0] = kv_in[targets[0]]
    recv_q[0] = q_in[targets[0]]

    for step in range(1, reps):
        exchange(step, 0, send_kv, recv_kv).wait_recv()
    slots = [source_slot(b) for b in range(blocks)]
    for b in range(blocks):
        kvs[z, place(core, b * BLOCK, BLOCK), :] = recv_kv[slots[b]]

    def hop(slot, half, part, device, send, recv, k):
        where = kvs.at[slot, place(half, *pieces[part]), :]
        return pltpu.make_async_remote_copy(
            src_ref=where, dst_ref=where, send_sem=send.at[k, part], recv_sem=recv.at[k, part],
            device_id=device, device_id_type=MESH,
        )

    def up(slot, part, k):
        return hop(slot, core, part, above, up_send, up_recv, k)

    def far(slot, part, device):
        return hop(slot, core, part, device, far_send, far_recv, slot)

    def sib(slot, part, k):
        return hop(slot, core, part, sibling, sib_send, sib_recv, k)

    def from_sib(slot, k):
        for part in range(PARTS):
            hop(slot, 1 - core, part, sibling, sib_send, sib_recv, k).wait_recv()

    @pl.when(z < last)
    def _():
        pl.semaphore_wait(ready.at[0], 1)
        for part in range(PARTS):
            up(z, part, 1).start()

    @pl.when((z == 1) | (z == 2))
    def _():
        for part in range(PARTS):
            far(z, part, on_chip(0)).start()

    @pl.when(core == 0)
    def _():
        for part in range(PARTS):
            sib(z, part, 0).start()

    def has_far(k):
        return ((k == 2) & (z >= last - 1)) | ((k == 3) & ((z == last) | (z == last - 2))) | ((k == 4) & (z == last - 1))

    def far_number(k):
        return jnp.where(k == 2, 1, 2)

    def far_slot(k):
        return jnp.maximum(z - last + far_number(k), 0)

    def take_up(k):
        slot = (z + chips - k) % chips

        @pl.when(z >= k)
        def _():
            for part in range(PARTS):
                up(slot, part, k).wait_recv()

                @pl.when((k < UP) & (z < last))
                def _():
                    up(slot, part, k + 1).start()

                sib(slot, part, k).start()

    def take_far(k):
        for part in range(PARTS):
            far(far_slot(k), part, below).wait_recv()

            @pl.when(k == 2)
            def _():
                far(far_slot(k), part, below).start()

            sib(far_slot(k), part, UP + far_number(k)).start()

    take_up(1)

    @pl.when(z == last - 1)
    def _():
        take_far(2)

    for step in range(1, reps):
        exchange(step, 1, send_q, recv_q).wait_recv()
    for b in range(blocks):
        q_block = recv_q[slots[b]]
        for h in range(heads):
            qa[h * rows + b * BLOCK : h * rows + (b + 1) * BLOCK, 0:HEAD] = q_block[:, h * HEAD : (h + 1) * HEAD]

    def unit(slot, halves, diagonal):
        key_rows, value_rows = [], []
        for half in halves:
            note = kvs[slot, place(half, rows, NOTE), :].astype(jnp.float32)
            note = note[0:1, :] + note[1:2, :]
            hide = jnp.where(within(note[:, 0:HEAD], note[:, HEAD:]), 0.0, HIDE).astype(jnp.bfloat16)
            keys = kvs[slot, place(half, 0, rows), 0:HEAD]
            values = kvs[slot, place(half, 0, rows), HEAD:]
            key_rows.append(jnp.concatenate([keys, hide], axis=1))
            value_rows.append(jnp.concatenate([values, jnp.ones_like(values)], axis=1))
        key_rows = jnp.concatenate(key_rows, axis=0)
        value_rows = jnp.concatenate(value_rows, axis=0)

        def score(h):
            s = lax.dot_general(
                qa[h * rows : (h + 1) * rows, :], key_rows, (((1,), (1,)), ((), ())),
                preferred_element_type=jnp.float32,
            )
            if diagonal:
                ahead = lax.broadcasted_iota(jnp.int32, s.shape, 1) > lax.broadcasted_iota(jnp.int32, s.shape, 0)
                s = jnp.where(ahead, HIDE, s)
            return s

        def soften(h, s):
            part = slice(h * rows, (h + 1) * rows)
            high = jnp.max(s, axis=1, keepdims=True)
            if diagonal:
                now = jnp.broadcast_to(high, (rows, HEAD))
                decay = None
            else:
                now = jnp.maximum(top[part, :], high)
                decay = jnp.exp2((top[part, :] - now) * SCALE)
            top[part, :] = now
            p = jnp.exp2((s - jnp.concatenate([now] * (s.shape[1] // HEAD), axis=1)) * SCALE)
            return p.astype(jnp.bfloat16), decay

        def mix(h, p, decay):
            part = slice(h * rows, (h + 1) * rows)
            o = jnp.dot(p, value_rows, preferred_element_type=jnp.float32)
            if diagonal:
                acc[part, :] = o
            else:
                acc[part, :] = acc[part, :] * jnp.concatenate([decay] * 2, axis=1) + o

        scores = {0: score(0)}
        soft = {}
        for h in range(heads + 1):
            if h + 1 < heads:
                scores[h + 1] = score(h + 1)
            if h < heads:
                soft[h] = soften(h, scores.pop(h))
            if h >= 1:
                mix(h - 1, *soft.pop(h - 1))

    unit(z, [core], True)

    @pl.when(z == 0)
    def _():
        pl.semaphore_wait(ready.at[1], 1)
        for part in range(PARTS):
            far(0, part, on_chip(last - 1)).start()
        pl.semaphore_wait(ready.at[2], 1)
        for slot in (1, 2):
            for part in range(PARTS):
                far(slot, part, on_chip(last)).wait_recv()
                far(slot, part, on_chip(last)).start()

    @pl.when(core == 1)
    def _():
        from_sib(z, 0)
        unit(z, [0], False)

    def receive(k, _):
        @pl.when(z >= k)
        def _():
            slot = (z + chips - k) % chips
            from_sib(slot, k)
            unit(slot, [0, 1], False)

        @pl.when(k < UP)
        def _():
            take_up(k + 1)

        @pl.when((k == 1) & (z == last))
        def _():
            take_far(2)

        @pl.when(has_far(k))
        def _():
            @pl.when(k > 2)
            def _():
                take_far(k)

            from_sib(far_slot(k), UP + far_number(k))
            unit(far_slot(k), [0, 1], False)

        return 0

    lax.fori_loop(1, UP + 1, receive, 0)

    for h in range(heads):
        part = slice(h * rows, (h + 1) * rows)
        out[:, h * HEAD : (h + 1) * HEAD] = (acc[part, 0:HEAD] / acc[part, HEAD:]).astype(jnp.bfloat16)
    result = pltpu.make_async_copy(out, out_hbm.at[0], out_sem)
    result.start()

    for step in range(1, reps):
        exchange(step, 0, send_kv, recv_kv).wait_send()
        exchange(step, 1, send_q, recv_q).wait_send()

    def drain(k, _):
        slot = (z + chips - k) % chips
        for part in range(PARTS):
            @pl.when(z >= k)
            def _():
                @pl.when((k < UP) & (z < last))
                def _():
                    up(slot, part, k + 1).wait_send()

                sib(slot, part, k).wait_send()

            @pl.when(has_far(k))
            def _():
                @pl.when(k == 2)
                def _():
                    far(far_slot(k), part, below).wait_send()

                sib(far_slot(k), part, UP + far_number(k)).wait_send()

        return 0

    lax.fori_loop(1, UP + 1, drain, 0)
    for part in range(PARTS):
        @pl.when(z < last)
        def _():
            up(z, part, 1).wait_send()

        @pl.when((z == 1) | (z == 2))
        def _():
            far(z, part, on_chip(0)).wait_send()

        @pl.when(z == 0)
        def _():
            for slot in range(3):
                far(slot, part, on_chip(last)).wait_send()

        @pl.when(core == 0)
        def _():
            sib(z, part, 0).wait_send()

    result.wait()


def body(q_arrived, key_value_landed, finish, document_numbers):
    rows, q_width = q_arrived.shape[1:]
    kv_width = key_value_landed.shape[2]
    reps = lax.axis_size("rep")
    ctxs = lax.axis_size("ctx")
    heads = q_width // HEAD
    blocks = rows // BLOCK
    bf16, f32 = jnp.bfloat16, jnp.float32
    dma = pltpu.SemaphoreType.DMA
    return pl.pallas_call(
        functools.partial(kernel, reps, ctxs),
        out_shape=jax.ShapeDtypeStruct(q_arrived.shape, bf16),
        in_specs=[pl.BlockSpec(memory_space=pl.ANY)] * 4,
        out_specs=pl.BlockSpec(memory_space=pl.ANY),
        scratch_shapes=[
            pltpu.VMEM((blocks, BLOCK, q_width), bf16),
            pltpu.VMEM((blocks, BLOCK, kv_width), bf16),
            pltpu.SMEM(finish.shape, jnp.int32),
            pltpu.VMEM(document_numbers.shape, jnp.int32),
            pltpu.VMEM((reps, BLOCK, kv_width), bf16),
            pltpu.VMEM((reps, BLOCK, q_width), bf16),
            pltpu.VMEM((reps, BLOCK, kv_width), bf16),
            pltpu.VMEM((reps, BLOCK, q_width), bf16),
            pltpu.VMEM((ctxs // 2, 2 * (rows + NOTE), kv_width), bf16),
            pltpu.VMEM((heads * rows, 2 * HEAD), bf16),
            pltpu.VMEM((heads * rows, HEAD), f32),
            pltpu.VMEM((heads * rows, 2 * HEAD), f32),
            pltpu.VMEM((rows, q_width), bf16),
            dma((4,)),
            dma((2, reps)),
            dma((2, reps)),
            pltpu.SemaphoreType.REGULAR((3,)),
            dma((UP + 1, PARTS)),
            dma((UP + 1, PARTS)),
            dma((3, PARTS)),
            dma((3, PARTS)),
            dma((UP + 3, PARTS)),
            dma((UP + 3, PARTS)),
            dma,
        ],
        compiler_params=pltpu.CompilerParams(
            collective_id=0, has_side_effects=True, vmem_limit_bytes=62 * 2**20
        ),
    )(
        q_arrived.reshape(blocks, BLOCK, q_width),
        key_value_landed.reshape(blocks, BLOCK, kv_width),
        finish,
        document_numbers,
    )


def solution(mesh):
    in_specs = (P("rep", "ctx", "tp"), P("rep", "ctx", "tp"), P("ctx", None), P("rep", "ctx"))
    out_specs = P("rep", "ctx", "tp")
    return jax.shard_map(body, mesh=mesh, in_specs=in_specs, out_specs=out_specs, check_vma=False)
```

time: 43.5 us -> 38.8 us (0.89)
  the two profiles are of different devices: /device:TPU:337 before, /device:TPU:453 now
where the time goes in v2:
time: 38.8 us; the launch traced here: 38.7 us
  Pallas kernels  36.9 us (95%)
  local copies, waits for them, and re-layouts  1.77 us (5%)
    pallas_call x1, Pallas kernels, body(): pl.pallas_call(functools.partial(kernel, reps, ctxs), out_shape=jax.Shape...  36.9 us
    unnamed x1, local copies, waits for them, and re-layouts  1.77 us

profile of v2, /device:TPU:453, one launch (start us, length us, event | category | flops | bytes accessed | tf_op | source)
XLA Modules:
  0.0 38.7 jit_solution(16894514052236895609)
XLA Ops:
  0.0 36.9 %shard_map.46 = bf16[1,384,512]{2,1,0:T(8,128)(2,1)} custom-call(bf16[3,128,512]{2,1,0:T(8,128)(2,1)} %bitcast.2, bf16[3,128,256]{2,1,0:T(8,128)(2,1)} %bitcast.3, s32[3,4]{1,0:T(4,128)} %fin_hbm.1, s32[1,384]{1,0:T(1,128)} %doc_hbm.1), custom_call_target="tpu_custom_call" | custom-call | tf_op jit(solution)/shard_map/pallas_call | solution.py:397
  36.9 1.8 %copy.6 = bf16[1,384,512]{2,1,0:T(8,128)(2,1)} copy(bf16[1,384,512]{2,1,0:T(8,128)(2,1)} %shard_map.46) | data formatting | bytes 786432

commit v3 on v2

--- a/solution.py
+++ b/solution.py
@@ -187,7 +187,9 @@
             sib(z, part, 0).start()
 
     def has_far(k):
-        return ((k == 2) & (z >= last - 1)) | ((k == 3) & ((z == last) | (z == last - 2))) | ((k == 4) & (z == last - 1))
+        first = (k == 2) & (z >= last - 1)
+        second = ((k == 3) & (z == last)) | ((k == 4) & ((z == last - 1) | (z == last - 2)))
+        return first | second
 
     def far_number(k):
         return jnp.where(k == 2, 1, 2)
@@ -221,9 +223,16 @@
 
     take_up(1)
 
-    @pl.when(z == last - 1)
-    def _():
-        take_far(2)
+    @pl.when(z == 0)
+    def _():
+        pl.semaphore_wait(ready.at[1], 1)
+        for part in range(PARTS):
+            far(0, part, on_chip(last - 1)).start()
+        pl.semaphore_wait(ready.at[2], 1)
+        for slot in (1, 2):
+            for part in range(PARTS):
+                far(slot, part, on_chip(last)).wait_recv()
+                far(slot, part, on_chip(last)).start()
 
     for step in range(1, reps):
         exchange(step, 1, send_q, recv_q).wait_recv()
@@ -288,45 +297,30 @@
 
     unit(z, [core], True)
 
-    @pl.when(z == 0)
-    def _():
-        pl.semaphore_wait(ready.at[1], 1)
-        for part in range(PARTS):
-            far(0, part, on_chip(last - 1)).start()
-        pl.semaphore_wait(ready.at[2], 1)
-        for slot in (1, 2):
-            for part in range(PARTS):
-                far(slot, part, on_chip(last)).wait_recv()
-                far(slot, part, on_chip(last)).start()
-
     @pl.when(core == 1)
     def _():
         from_sib(z, 0)
         unit(z, [0], False)
 
     def receive(k, _):
+        @pl.when(has_far(k))
+        def _():
+            take_far(k)
+
         @pl.when(z >= k)
         def _():
             slot = (z + chips - k) % chips
             from_sib(slot, k)
             unit(slot, [0, 1], False)
 
-        @pl.when(k < UP)
-        def _():
-            take_up(k + 1)
-
-        @pl.when((k == 1) & (z == last))
-        def _():
-            take_far(2)
-
         @pl.when(has_far(k))
         def _():
-            @pl.when(k > 2)
-            def _():
-                take_far(k)
-
             from_sib(far_slot(k), UP + far_number(k))
             unit(far_slot(k), [0, 1], False)
+
+        @pl.when(k < UP)
+        def _():
+            take_up(k + 1)
 
         return 0
 

time: 38.8 us -> 37.7 us (0.972)
  the two profiles are of different devices: /device:TPU:453 before, /device:TPU:439 now
where the time goes in v3:
time: 37.7 us; the launch traced here: 37.5 us
  Pallas kernels  35.7 us (95%)
  local copies, waits for them, and re-layouts  1.77 us (5%)
    pallas_call x1, Pallas kernels, body(): pl.pallas_call(functools.partial(kernel, reps, ctxs), out_shape=jax.Shape...  35.7 us
    unnamed x1, local copies, waits for them, and re-layouts  1.77 us

profile of v3, /device:TPU:439, one launch (start us, length us, event | category | flops | bytes accessed | tf_op | source)
XLA Modules:
  0.0 37.5 jit_solution(7147627253873477738)
XLA Ops:
  0.0 35.7 %shard_map.46 = bf16[1,384,512]{2,1,0:T(8,128)(2,1)} custom-call(bf16[3,128,512]{2,1,0:T(8,128)(2,1)} %bitcast.2, bf16[3,128,256]{2,1,0:T(8,128)(2,1)} %bitcast.3, s32[3,4]{1,0:T(4,128)} %fin_hbm.1, s32[1,384]{1,0:T(1,128)} %doc_hbm.1), custom_call_target="tpu_custom_call" | custom-call | tf_op jit(solution)/shard_map/pallas_call | solution.py:391
  35.7 1.8 %copy.6 = bf16[1,384,512]{2,1,0:T(8,128)(2,1)} copy(bf16[1,384,512]{2,1,0:T(8,128)(2,1)} %shard_map.46) | data formatting | bytes 786432

commit v4 on v3

--- a/solution.py
+++ b/solution.py
@@ -313,24 +313,26 @@
             from_sib(slot, k)
             unit(slot, [0, 1], False)
 
+        @pl.when(k < UP)
+        def _():
+            take_up(k + 1)
+
         @pl.when(has_far(k))
         def _():
             from_sib(far_slot(k), UP + far_number(k))
             unit(far_slot(k), [0, 1], False)
 
-        @pl.when(k < UP)
-        def _():
-            take_up(k + 1)
-
         return 0
 
     lax.fori_loop(1, UP + 1, receive, 0)
 
+    results = []
     for h in range(heads):
         part = slice(h * rows, (h + 1) * rows)
-        out[:, h * HEAD : (h + 1) * HEAD] = (acc[part, 0:HEAD] / acc[part, HEAD:]).astype(jnp.bfloat16)
-    result = pltpu.make_async_copy(out, out_hbm.at[0], out_sem)
-    result.start()
+        columns = slice(h * HEAD, (h + 1) * HEAD)
+        out[:, columns] = (acc[part, 0:HEAD] / acc[part, HEAD:]).astype(jnp.bfloat16)
+        results.append(pltpu.make_async_copy(out.at[:, columns], out_hbm.at[0, :, columns], out_sem.at[h]))
+        results[h].start()
 
     for step in range(1, reps):
         exchange(step, 0, send_kv, recv_kv).wait_send()
@@ -376,7 +378,8 @@
         def _():
             sib(z, part, 0).wait_send()
 
-    result.wait()
+    for result in results:
+        result.wait()
 
 
 def body(q_arrived, key_value_landed, finish, document_numbers):
@@ -417,7 +420,7 @@
             dma((3, PARTS)),
             dma((UP + 3, PARTS)),
             dma((UP + 3, PARTS)),
-            dma,
+            dma((heads,)),
         ],
         compiler_params=pltpu.CompilerParams(
             collective_id=0, has_side_effects=True, vmem_limit_bytes=62 * 2**20

time: 37.7 us -> 37.7 us (level)
  no operation moved by 1% of the time
where the time goes in v4:
time: 37.7 us; the launch traced here: 37.5 us
  Pallas kernels  35.7 us (95%)
  local copies, waits for them, and re-layouts  1.77 us (5%)
    pallas_call x1, Pallas kernels, body(): pl.pallas_call(functools.partial(kernel, reps, ctxs), out_shape=jax.Shape...  35.7 us
    unnamed x1, local copies, waits for them, and re-layouts  1.77 us

profile of v4, /device:TPU:439, one launch (start us, length us, event | category | flops | bytes accessed | tf_op | source)
XLA Modules:
  0.0 37.5 jit_solution(3681971294108598919)
XLA Ops:
  0.0 35.7 %shard_map.46 = bf16[1,384,512]{2,1,0:T(8,128)(2,1)} custom-call(bf16[3,128,512]{2,1,0:T(8,128)(2,1)} %bitcast.2, bf16[3,128,256]{2,1,0:T(8,128)(2,1)} %bitcast.3, s32[3,4]{1,0:T(4,128)} %fin_hbm.1, s32[1,384]{1,0:T(1,128)} %doc_hbm.1), custom_call_target="tpu_custom_call" | custom-call | tf_op jit(solution)/shard_map/pallas_call | solution.py:394
  35.7 1.8 %copy.6 = bf16[1,384,512]{2,1,0:T(8,128)(2,1)} copy(bf16[1,384,512]{2,1,0:T(8,128)(2,1)} %shard_map.46) | data formatting | bytes 786432
